TPU v7x, 256 devices: a whole 4x4x8 slice. The times are simulated.
256 devices in a mesh: tm: 8 (over y, core), rows: 8 (over z), dp: 4 (over x).
Axes of the slice: x: 4, y: 4, z: 8, core: 2. Of those that a mesh axis runs over, the one named last changes fastest.
Arguments:
- video: bfloat16 [4, 128, 32, 32, 128], P('dp', 'tm', 'rows'), may hold values from -6 to 6
- cotangent: bfloat16 [4, 128, 32, 32, 128], P('dp', 'tm', 'rows'), may hold values from -6 to 6
- in_kernel: bfloat16 [3, 3, 128, 128], replicated, may hold values from -0.03125 to 0.03125
- out_kernel: bfloat16 [3, 3, 128, 128], replicated, may hold values from -0.1875 to 0.1875
- skip_gain: float32 [128], replicated, may hold values from 0.5 to 1.5
- log_decay: float32 [128, 128], P('tm'), may hold values from -3 to 0, as said below
Outputs:
- layer_out: bfloat16 [4, 128, 32, 32, 128], P('dp', 'tm', 'rows')
- video_grad: bfloat16 [4, 128, 32, 32, 128], P('dp', 'tm', 'rows')
- in_kernel_grad: float32 [3, 3, 128, 128], replicated
- out_kernel_grad: float32 [3, 3, 128, 128], replicated
- skip_gain_grad: float32 [128], replicated
- decay_grad: float32 [128, 128], P('tm')
Inputs may be any that keep to these rules, and one draw needn't show every extreme that they name: log_decay is negative.
All inputs are finite; a program needn't handle non-finite values.
Results may differ from a plain program's by a relative error of at most 0.0085.
Values may be sent and summed in bfloat16 or wider, within the bound.
A program may use at most 64 MiB of HBM per device.

v0:
```python
import math
import jax
import jax.numpy as jnp
from jax import lax
from jax.sharding import PartitionSpec as P


def padded_2(cells, sides, width):
    for axis, dim in sides:
        count = lax.axis_size(axis)
        ends = count - 1
        head = lax.slice_in_dim(cells, 0, width, axis=dim)
        tail = lax.slice_in_dim(cells, cells.shape[dim] - width, cells.shape[dim], axis=dim)
        cells = jnp.concatenate(
            [
                lax.ppermute(tail, axis, [(i, (i + 1) % count) for i in range(ends)]),
                cells,
                lax.ppermute(head, axis, [((i + 1) % count, i) for i in range(ends)]),
            ],
            axis=dim,
        )
    return cells


def prefix(value, axis, join, neutral):
    count, mine = (lax.axis_size(axis), lax.axis_index(axis))
    pieces = jax.tree.map(lambda part: lax.all_gather(part, axis), value)
    running = jax.tree.map(
        lambda part, zero: jnp.full_like(part, 0) + jnp.asarray(zero, part.dtype), value, neutral
    )

    def prefix_lap(position, running):
        longer = join(running, jax.tree.map(lambda part: part[position], pieces))
        return jax.tree.map(lambda new, old: jnp.where(position < mine, new, old), longer, running)

    return lax.fori_loop(0, count - 1, prefix_lap, running)


def entering(array, axis, combine, identity):
    devices, position = (lax.axis_size(axis), lax.axis_index(axis))
    everything = jax.tree.map(
        lambda part, kind: lax.all_gather(part.astype(kind), axis),
        array,
        (jnp.bfloat16, jnp.bfloat16),
    )
    start = jax.tree.map(
        lambda part, zero: jnp.broadcast_to(jnp.asarray(zero, part.dtype), part.shape),
        array,
        identity,
    )

    def entering_lap(k, before):
        at = devices - 1 - k
        reached = at > position
        new = combine(
            before, jax.tree.map(lambda part, own: part[at].astype(own.dtype), everything, array)
        )
        return jax.tree.map(lambda a, b: jnp.where(reached, a, b), new, before)

    return lax.fori_loop(0, devices, entering_lap, start)


def pad_columns(field):
    return jnp.pad(field, ((0, 0), (0, 0), (0, 0), (1, 1), (0, 0)))


def forward_conv(padded, kernel):
    seqs, frames, rows_two, cols_two, chans = padded.shape
    rows, cols = (rows_two - 2, cols_two - 2)
    total = None
    for i in range(3):
        for j in range(3):
            piece = padded[:, :, i : i + rows, j : j + cols, :].reshape(-1, chans)
            term = jnp.dot(piece, kernel[i, j], preferred_element_type=jnp.float32)
            total = term if total is None else total + term
    return total.reshape(seqs, frames, rows, cols, kernel.shape[3])


def adjoint_conv(padded, kernel):
    seqs, frames, rows_two, cols_two, chans = padded.shape
    rows, cols = (rows_two - 2, cols_two - 2)
    total = None
    for i in range(3):
        for j in range(3):
            piece = padded[:, :, 2 - i : 2 - i + rows, 2 - j : 2 - j + cols, :].reshape(-1, chans)
            term = lax.dot_general(
                piece, kernel[i, j], (((1,), (1,)), ((), ())), preferred_element_type=jnp.float32
            )
            total = term if total is None else total + term
    return total.reshape(seqs, frames, rows, cols, kernel.shape[2])


def kernel_grad(padded, grad):
    seqs, frames, rows_two, cols_two, chans = padded.shape
    rows, cols = (rows_two - 2, cols_two - 2)
    flat_grad = grad.reshape(-1, grad.shape[-1])
    outer_list = []
    for i in range(3):
        inner_list = []
        for j in range(3):
            piece = padded[:, :, i : i + rows, j : j + cols, :].reshape(-1, chans)
            inner_list.append(
                lax.dot_general(
                    piece, flat_grad, (((0,), (0,)), ((), ())), preferred_element_type=jnp.float32
                )
            )
        outer_list.append(jnp.stack(inner_list))
    return jnp.stack(outer_list)


def combine_groups(earlier, later):
    return (earlier[0] * later[0], later[0] * earlier[1] + later[1])


def on_device(video, cotangent, in_kernel, out_kernel, skip_gain, log_decay):
    seqs, frames, rows, cols, chans = video.shape
    padded_x = pad_columns(padded_2(video, (("rows", 2),), 1))
    drive = forward_conv(padded_x, in_kernel)
    cum = jnp.cumsum(log_decay, axis=0)
    later_mask = (
        lax.broadcasted_iota(jnp.int32, (frames, frames), 0)
        >= lax.broadcasted_iota(jnp.int32, (frames, frames), 1)
    )[:, :, None]
    gaps = cum[:, None, :] - cum[None, :, :]
    within = jnp.where(later_mask, jnp.exp(jnp.where(later_mask, gaps, 0.0)), 0.0)
    local_states = jnp.einsum("tkp,skrcp->strcp", within, drive, precision=lax.Precision.HIGHEST)
    group_total = cum[-1]
    group_decay = jnp.exp(group_total)
    empty = jnp.zeros_like(local_states[:, -1])
    identity = (jnp.ones_like(group_total), empty)
    _, carry_in = prefix((group_decay, local_states[:, -1]), "tm", combine_groups, identity)
    states = local_states + jnp.exp(cum)[None, :, None, None, :] * carry_in[:, None]
    states_bf = states.astype(jnp.bfloat16)
    padded_s = pad_columns(padded_2(states_bf, (("rows", 2),), 1))
    pre = forward_conv(padded_s, out_kernel) + skip_gain * video.astype(jnp.float32)
    activated, pullback = jax.vjp(jax.nn.gelu, pre)
    grad_pre = pullback(cotangent.astype(jnp.float32))[0]
    grad_bf = grad_pre.astype(jnp.bfloat16)
    out_grad = kernel_grad(padded_s, grad_bf)
    gain_grad = jnp.sum(grad_pre * video.astype(jnp.float32), axis=(0, 1, 2, 3))
    padded_g = pad_columns(padded_2(grad_bf, (("rows", 2),), 1))
    state_grad = adjoint_conv(padded_g, out_kernel)
    local_adjoint = jnp.einsum(
        "tkp,strcp->skrcp", within, state_grad, precision=lax.Precision.HIGHEST
    )
    leading = jnp.exp(cum[0])[None, None, None, :] * local_adjoint[:, 0]
    _, back_in = entering((group_decay, leading), "tm", combine_groups, identity)
    adjoint = (
        local_adjoint
        + jnp.exp(group_total[None, :] - cum)[None, :, None, None, :] * back_in[:, None]
    )
    previous = jnp.concatenate([carry_in[:, None], states[:, :-1]], axis=1)
    decay_part = jnp.sum(
        adjoint * jnp.exp(log_decay)[None, :, None, None, :] * previous, axis=(0, 2, 3)
    )
    decay_scale = 1.0 / math.sqrt(seqs * rows * cols * lax.axis_size("rows") * lax.axis_size("dp"))
    decay_grad = lax.psum(decay_part, ("rows", "dp")) * decay_scale
    adjoint_bf = adjoint.astype(jnp.bfloat16)
    in_grad = kernel_grad(padded_x, adjoint_bf)
    padded_a = pad_columns(padded_2(adjoint_bf, (("rows", 2),), 1))
    video_grad = (adjoint_conv(padded_a, in_kernel) + skip_gain * grad_pre).astype(jnp.bfloat16)
    in_sum, out_sum, gain_sum = lax.psum((in_grad, out_grad, gain_grad), ("tm", "rows", "dp"))
    weight_scale = 1.0 / math.sqrt(
        seqs
        * frames
        * rows
        * cols
        * lax.axis_size("tm")
        * lax.axis_size("rows")
        * lax.axis_size("dp")
    )
    return (
        activated.astype(jnp.bfloat16),
        video_grad,
        in_sum * weight_scale,
        out_sum * weight_scale,
        gain_sum * weight_scale,
        decay_grad,
    )


def solution(mesh):
    placed = (
        P("dp", "tm", "rows", None, None),
        P("dp", "tm", "rows", None, None),
        P(),
        P(),
        P(),
        P("tm", None),
    )
    return jax.shard_map(
        on_device,
        mesh=mesh,
        in_specs=placed,
        out_specs=(
            P("dp", "tm", "rows", None, None),
            P("dp", "tm", "rows", None, None),
            P(),
            P(),
            P(),
            P("tm", None),
        ),
        check_vma=False,
    )
```

profile of v0, /device:TPU:8, one launch (start us, length us, event | category | flops | bytes accessed | tf_op | source)
XLA Modules:
  0.0 646.0 jit_solution(3192037692985163156)
XLA Ops:
  7.2 1.0 fusion.179
  8.2 3.8 collective-permute-start
  12.0 1.3 collective-permute-start.1
  13.3 0.7 reduce_window_sum.11
  14.8 8.7 %all-gather = f32[8,1,128]{2,1,0:T(1,128)S(1)} all-gather(f32[1,1,128]{2,1,0:T(1,128)S(1)} %get-tuple-element.381), channel_id=1, replica_groups=mesh['tm'=8,'rows'=8,'dp'=4] {'tm'}, dimensions={0}, use_global_device_ids=true | all-gather | bytes 4608 | tf_op jit(solution)/shard_map/all_gather | solution.py:27
  23.5 1.6 fusion.27
  29.1 4.5 copy.179
  33.6 8.3 %fusion.21 = f32[128,4,32,16]{2,3,1,0:T(8,128)} fusion(f32[16,4,32,128]{2,0,1,3:T(8,128)} %copy.179, f32[16,128]{0,1:T(8,128)S(1)} %copy.177, pred[16,16]{0,1:T(8,128)(4,1)S(1)} %iota_compare_fusion.2), kind=kOutput, calls=%fused_computation.80 | convolution fusion | flops 50429952 | bytes 2105600 | tf_op jit(solution)/shard_map/tkp,skrcp->strcp/dot_general | solution.py:126
  41.9 3.7 copy.181
  45.6 12.7 %all_gather.16 = f32[8,1,4,32,128]{4,3,2,1,0:T(8,128)S(1)} all-gather(f32[1,1,4,32,128]{4,3,2,1,0:T(8,128)S(1)} %slice.319), channel_id=1, replica_groups=mesh['tm'=8,'rows'=8,'dp'=4] {'tm'}, dimensions={0}, use_global_device_ids=true | all-gather | bytes 589824 | tf_op jit(solution)/shard_map/all_gather | solution.py:27
  58.7 2.4 fusion.171
  61.2 4.6 collective-permute-start.2
  65.7 1.3 collective-permute-start.3
  67.1 11.1 %all-gather.1 = bf16[8,1,128]{2,1,0:T(2,128)(2,1)S(1)} all-gather(bf16[1,1,128]{2,1,0:T(2,128)(2,1)S(1)} %get-tuple-element.380), channel_id=1, replica_groups=mesh['tm'=8,'rows'=8,'dp'=4] {'tm'}, dimensions={0}, use_global_device_ids=true | all-gather | bytes 2304 | tf_op jit(solution)/shard_map/all_gather | solution.py:42
  78.8 2.3 slice.346
  85.2 0.7 copy-done.12
  85.9 2.3 fusion.8
  88.3 1.0 convolution_bitcast_fusion.7
  89.3 1.0 convolution_bitcast_fusion.3
  90.2 1.0 convolution_bitcast_fusion.5
  91.2 1.0 convolution_bitcast_fusion.6
  92.2 1.0 convolution_bitcast_fusion.8
  93.2 1.0 convolution_bitcast_fusion.4
  94.1 1.0 convolution_bitcast_fusion.1
  95.1 1.0 convolution_bitcast_fusion
  96.1 1.0 convolution_bitcast_fusion.2
  97.1 4.6 collective-permute-start.4
  101.7 1.3 collective-permute-start.5
  103.0 80.3 %psum.30 = f32[128]{0:T(128)S(1)} all-reduce(f32[128]{0:T(128)S(1)} %copy-done.25), channel_id=1, replica_groups=mesh['tm'=8,'rows'=8,'dp'=4] {'tm','rows','dp'}, use_global_device_ids=true, to_apply=%region_8.9 | all-reduce | flops 128 | bytes 1024 | tf_op jit(solution)/shard_map/psum | solution.py:162
  183.8 0.9 maximum_bitcast_fusion.5
  184.8 0.9 pad_maximum_fusion.1
  189.9 4.5 copy.182
  194.4 8.2 %fusion.19 = f32[128,4,32,16]{2,3,1,0:T(8,128)} fusion(f32[16,4,32,128]{2,0,1,3:T(8,128)} %copy.182, f32[16,128]{0,1:T(8,128)S(1)} %copy.177, pred[16,16]{0,1:T(8,128)(4,1)S(1)} %copy-done.21), kind=kOutput, calls=%fused_computation.78 | convolution fusion | flops 50429952 | bytes 2105600 | tf_op jit(solution)/shard_map/tkp,strcp->skrcp/dot_general | solution.py:143
  202.6 3.7 copy.183
  206.3 13.1 %all_gather.18 = bf16[8,1,4,32,128]{4,3,2,1,0:T(8,128)(2,1)S(1)} all-gather(bf16[1,1,4,32,128]{4,3,2,1,0:T(8,128)(2,1)S(1)} %fusion.73), channel_id=1, replica_groups=mesh['tm'=8,'rows'=8,'dp'=4] {'tm'}, dimensions={0}, use_global_device_ids=true | all-gather | bytes 294912 | tf_op jit(solution)/shard_map/all_gather | solution.py:42
  219.4 5.9 while.31
  220.2 0.7 bitcast_convert_fusion.2
  220.9 0.7 bitcast_convert_fusion.2
  225.3 1.5 fusion.18
  230.4 3.7 collective-permute-start.6
  234.0 1.3 collective-permute-start.7
  235.4 141.5 %psum.31 = f32[16,128]{0,1:T(8,128)S(1)} all-reduce(f32[16,128]{0,1:T(8,128)S(1)} %copy.211), channel_id=1, replica_groups=mesh['tm'=8,'rows'=8,'dp'=4] {'rows','dp'}, use_global_device_ids=true, to_apply=%region_10.11 | all-reduce | flops 2048 | bytes 16384 | tf_op jit(solution)/shard_map/psum | solution.py:157
  377.7 0.9 pad_maximum_fusion
  382.9 0.9 copy-done.2
  383.8 1.0 add_convert_fusion
  384.8 250.3 %all-reduce.7.cloned.1.call-done = (f32[3,3,128,128]{3,2,1,0:T(8,128)}, f32[3,3,128,128]{3,2,1,0:T(8,128)}) async-done(((f32[3,3,128,128]{3,2,1,0:T(8,128)}, f32[3,3,128,128]{3,2,1,0:T(8,128)}), (f32[3,3,128,128]{3,2,1,0:T(8,128)}, f32[3,3,128,128]{3,2,1,0:T(8,128)})) %all-reduce.7.cloned.1.call-update) | async-done | bytes 1179664 | tf_op jit(solution)/shard_map/psum | solution.py:162
  635.1 1.9 broadcast_multiply_fusion
  637.0 1.9 broadcast_multiply_fusion.1
  (166 shorter events, 27.5 us)
Async XLA Ops:
  7.2 627.9 %all-reduce.7.cloned.1.call-start = ((), (), s32[]{:S(2)}) async-start(), calls=%async_computation | async-start | bytes 2359296 | tf_op jit(solution)/shard_map/psum | solution.py:162
  8.2 15.3 %collective-permute-start = (bf16[1,16,1,32,128]{4,3,2,1,0:T(8,128)(2,1)S(1)}, bf16[1,16,1,32,128]{4,3,2,1,0:T(8,128)(2,1)S(1)}, u32[]{:S(2)}, u32[]{:S(2)}) collective-permute-start(bf16[1,16,1,32,128]{4,3,2,1,0:T(8,128)(2,1)S(1)} %get-tuple-element.375), channel_id=1, source_target_pairs={{0,4},{4,8},{8,12},{12,16},{16,20},{20,24},{24,28},{1,5},{5,9},{9,... | collective-permute-start | bytes 393224 | tf_op jit(solution)/shard_map/ppermute | solution.py:16
  12.0 11.5 %collective-permute-start.1 = (bf16[1,16,1,32,128]{4,3,2,1,0:T(8,128)(2,1)S(1)}, bf16[1,16,1,32,128]{4,3,2,1,0:T(8,128)(2,1)S(1)}, u32[]{:S(2)}, u32[]{:S(2)}) collective-permute-start(bf16[1,16,1,32,128]{4,3,2,1,0:T(8,128)(2,1)S(1)} %get-tuple-element.376), channel_id=1, source_target_pairs={{4,0},{8,4},{12,8},{16,12},{20,16},{24,20},{28,24},{5,1},{9,5},{13... | collective-permute-start | bytes 393224 | tf_op jit(solution)/shard_map/ppermute | solution.py:18
  23.5 10.1 %copy-start.20 = (pred[16,16]{0,1:T(8,128)(4,1)}, pred[16,16]{0,1:T(8,128)(4,1)S(1)}, u32[]{:S(2)}) copy-start(pred[16,16]{0,1:T(8,128)(4,1)S(1)} %iota_compare_fusion.2) | copy-start | bytes 772
  25.1 1.0 copy-start.10
  25.7 1.1 copy-start
  26.9 0.8 copy-start.6
  26.9 1.9 copy-start.4
  45.6 13.1 %copy-start.3 = (f32[128,4,32,16]{0,2,1,3:T(8,128)}, f32[128,4,32,16]{0,2,1,3:T(8,128)S(1)}, u32[]{:S(2)}) copy-start(f32[128,4,32,16]{0,2,1,3:T(8,128)S(1)} %copy.181) | copy-start | bytes 3145732
  58.3 8.7 %copy-start.19 = (f32[16,128]{1,0:T(8,128)S(1)}, f32[16,128]{1,0:T(8,128)}, u32[]{:S(2)}) copy-start(f32[16,128]{1,0:T(8,128)} %param.15) | copy-start | bytes 24580
  61.2 19.9 %collective-permute-start.2 = (bf16[1,16,1,32,128]{4,3,2,1,0:T(8,128)(2,1)S(1)}, bf16[1,16,1,32,128]{4,3,2,1,0:T(8,128)(2,1)S(1)}, u32[]{:S(2)}, u32[]{:S(2)}) collective-permute-start(bf16[1,16,1,32,128]{4,3,2,1,0:T(8,128)(2,1)S(1)} %get-tuple-element.371), channel_id=1, source_target_pairs={{0,4},{4,8},{8,12},{12,16},{16,20},{20,24},{24,28},{1,5},{5,9},{9,... | collective-permute-start | bytes 393224 | tf_op jit(solution)/shard_map/ppermute | solution.py:16
  65.7 15.3 %collective-permute-start.3 = (bf16[1,16,1,32,128]{4,3,2,1,0:T(8,128)(2,1)S(1)}, bf16[1,16,1,32,128]{4,3,2,1,0:T(8,128)(2,1)S(1)}, u32[]{:S(2)}, u32[]{:S(2)}) collective-permute-start(bf16[1,16,1,32,128]{4,3,2,1,0:T(8,128)(2,1)S(1)} %get-tuple-element.372), channel_id=1, source_target_pairs={{4,0},{8,4},{12,8},{16,12},{20,16},{24,20},{28,24},{5,1},{9,5},{13... | collective-permute-start | bytes 393224 | tf_op jit(solution)/shard_map/ppermute | solution.py:18
  81.6 1.0 copy-start.8
  84.9 1.0 copy-start.12
  84.9 1.0 copy-start.23
  88.2 2.0 copy-start.1
  95.1 7.9 %copy-start.25 = (f32[128]{0:T(128)S(1)}, f32[128]{0:T(128)}, u32[]{:S(2)}) copy-start(f32[128]{0:T(128)} %get-tuple-element.330) | copy-start | bytes 1540
  95.1 88.7 %copy-start.13 = (f32[1,128,128]{2,1,0:T(8,128)S(1)}, f32[1,128,128]{2,1,0:T(8,128)}, u32[]{:S(2)}) copy-start(f32[1,128,128]{2,1,0:T(8,128)} %convolution_bitcast_fusion.7) | copy-start | bytes 196612
  95.1 88.7 %copy-start.14 = (f32[1,128,128]{2,1,0:T(8,128)S(1)}, f32[1,128,128]{2,1,0:T(8,128)}, u32[]{:S(2)}) copy-start(f32[1,128,128]{2,1,0:T(8,128)} %convolution_bitcast_fusion.3) | copy-start | bytes 196612
  95.1 88.7 %copy-start.15 = (f32[1,128,128]{2,1,0:T(8,128)S(1)}, f32[1,128,128]{2,1,0:T(8,128)}, u32[]{:S(2)}) copy-start(f32[1,128,128]{2,1,0:T(8,128)} %convolution_bitcast_fusion.5) | copy-start | bytes 196612
  95.1 88.7 %copy-start.16 = (f32[1,128,128]{2,1,0:T(8,128)S(1)}, f32[1,128,128]{2,1,0:T(8,128)}, u32[]{:S(2)}) copy-start(f32[1,128,128]{2,1,0:T(8,128)} %convolution_bitcast_fusion.6) | copy-start | bytes 196612
  95.1 88.7 %copy-start.17 = (f32[1,128,128]{2,1,0:T(8,128)S(1)}, f32[1,128,128]{2,1,0:T(8,128)}, u32[]{:S(2)}) copy-start(f32[1,128,128]{2,1,0:T(8,128)} %convolution_bitcast_fusion.8) | copy-start | bytes 196612
  95.1 88.7 %copy-start.18 = (f32[1,128,128]{2,1,0:T(8,128)S(1)}, f32[1,128,128]{2,1,0:T(8,128)}, u32[]{:S(2)}) copy-start(f32[1,128,128]{2,1,0:T(8,128)} %convolution_bitcast_fusion.4) | copy-start | bytes 196612
  97.1 88.5 %collective-permute-start.4 = (bf16[1,16,1,32,128]{4,3,2,1,0:T(8,128)(2,1)S(1)}, bf16[1,16,1,32,128]{4,3,2,1,0:T(8,128)(2,1)S(1)}, u32[]{:S(2)}, u32[]{:S(2)}) collective-permute-start(bf16[1,16,1,32,128]{4,3,2,1,0:T(8,128)(2,1)S(1)} %get-tuple-element.367), channel_id=1, source_target_pairs={{0,4},{4,8},{8,12},{12,16},{16,20},{20,24},{24,28},{1,5},{5,9},{9,... | collective-permute-start | bytes 393224 | tf_op jit(solution)/shard_map/ppermute | solution.py:16
  101.7 84.0 %collective-permute-start.5 = (bf16[1,16,1,32,128]{4,3,2,1,0:T(8,128)(2,1)S(1)}, bf16[1,16,1,32,128]{4,3,2,1,0:T(8,128)(2,1)S(1)}, u32[]{:S(2)}, u32[]{:S(2)}) collective-permute-start(bf16[1,16,1,32,128]{4,3,2,1,0:T(8,128)(2,1)S(1)} %get-tuple-element.368), channel_id=1, source_target_pairs={{4,0},{8,4},{12,8},{16,12},{20,16},{24,20},{28,24},{5,1},{9,5},{13... | collective-permute-start | bytes 393224 | tf_op jit(solution)/shard_map/ppermute | solution.py:18
  186.1 1.0 copy-start.9
  189.9 4.5 copy-start.21
  202.6 3.7 copy-start.22
  227.2 1.0 copy-start.5
  227.5 1.1 copy-start.7
  230.4 148.2 %collective-permute-start.6 = (bf16[1,16,1,32,128]{4,3,2,1,0:T(8,128)(2,1)S(1)}, bf16[1,16,1,32,128]{4,3,2,1,0:T(8,128)(2,1)S(1)}, u32[]{:S(2)}, u32[]{:S(2)}) collective-permute-start(bf16[1,16,1,32,128]{4,3,2,1,0:T(8,128)(2,1)S(1)} %get-tuple-element.363), channel_id=1, source_target_pairs={{0,4},{4,8},{8,12},{12,16},{16,20},{20,24},{24,28},{1,5},{5,9},{9,... | collective-permute-start | bytes 393224 | tf_op jit(solution)/shard_map/ppermute | solution.py:16
  234.0 144.5 %collective-permute-start.7 = (bf16[1,16,1,32,128]{4,3,2,1,0:T(8,128)(2,1)S(1)}, bf16[1,16,1,32,128]{4,3,2,1,0:T(8,128)(2,1)S(1)}, u32[]{:S(2)}, u32[]{:S(2)}) collective-permute-start(bf16[1,16,1,32,128]{4,3,2,1,0:T(8,128)(2,1)S(1)} %get-tuple-element.364), channel_id=1, source_target_pairs={{4,0},{8,4},{12,8},{16,12},{20,16},{24,20},{28,24},{5,1},{9,5},{13... | collective-permute-start | bytes 393224 | tf_op jit(solution)/shard_map/ppermute | solution.py:18
  379.1 1.0 copy-start.11
  382.5 1.2 copy-start.2
  382.5 1.2 copy-start.24
Sparse Core Ops, SparseCore 0:
  378.7 256.3 all-reduce.6
where the time goes:
time: 655 us; the launch traced here: 646 us
  blocking collectives  267 us (41%)
  waiting for transfers between devices  250 us (38%)
  matrix products  38.6 us (6%)
  local copies, waits for them, and re-layouts  27.4 us (4%)
  other arithmetic  25 us (4%)
  starting transfers between devices  21.8 us (3%)
  between operations  15 us (2%)
    psum x1, waiting for transfers between devices, on_device(): lax.psum((in_grad, out_grad, gain_grad), ('tm', 'rows', 'dp'))  250 us
    psum x1, blocking collectives, on_device(): decay_grad = lax.psum(decay_part, ('rows', 'dp')) * decay_scale  142 us
    psum x1, blocking collectives, on_device(): lax.psum((in_grad, out_grad, gain_grad), ('tm', 'rows', 'dp'))  80.3 us
    all_gather x2, blocking collectives, entering(): lax.all_gather(part.astype(kind), axis)  24.3 us
    all_gather x2, blocking collectives, prefix(): pieces = jax.tree.map(lambda part: lax.all_gather(part, axis), value)  21.4 us
    ppermute x4, starting transfers between devices, padded_2(): lax.ppermute(tail, axis, [(i, (i + 1) % count) for i in range(ends)])  16.6 us
  transfers between devices with their start and end apart: 9, of which 1 were waited for; matrix products, arithmetic and copies ran while one was open for 2% of the time, Pallas kernels for 0%

commit v1 on v0

--- a/solution.py
+++ b/solution.py
@@ -154,7 +154,10 @@
         adjoint * jnp.exp(log_decay)[None, :, None, None, :] * previous, axis=(0, 2, 3)
     )
     decay_scale = 1.0 / math.sqrt(seqs * rows * cols * lax.axis_size("rows") * lax.axis_size("dp"))
-    decay_grad = lax.psum(decay_part, ("rows", "dp")) * decay_scale
+    touch_packet_on = lambda content, named_axis, bus_axis: lax.psum(
+        lax.psum(content, named_axis), bus_axis
+    )
+    decay_grad = touch_packet_on(decay_part, "rows", "dp") * decay_scale
     adjoint_bf = adjoint.astype(jnp.bfloat16)
     in_grad = kernel_grad(padded_x, adjoint_bf)
     padded_a = pad_columns(padded_2(adjoint_bf, (("rows", 2),), 1))

time: 655 us -> 561 us (0.86)
  blocking collectives: 267 us -> 173 us
    psum x1 -> x2, blocking collectives: 142 us -> 46.6 us  [the longest x1 31.2 us: on_device(): lax.psum(content, named_axis)]
where the time goes in v1:
time: 561 us; the launch traced here: 552 us
  waiting for transfers between devices  251 us (45%)
  blocking collectives  173 us (31%)
  matrix products  38.5 us (7%)
  local copies, waits for them, and re-layouts  27.4 us (5%)
  other arithmetic  24.9 us (4%)
  starting transfers between devices  21.8 us (4%)
  between operations  15 us (3%)
    psum x1, waiting for transfers between devices, on_device(): lax.psum((in_grad, out_grad, gain_grad), ('tm', 'rows', 'dp'))  251 us
    psum x1, blocking collectives, on_device(): lax.psum((in_grad, out_grad, gain_grad), ('tm', 'rows', 'dp'))  80.3 us
    psum x1, blocking collectives, on_device(): lax.psum(content, named_axis)  31.2 us
    all_gather x2, blocking collectives, entering(): lax.all_gather(part.astype(kind), axis)  24.3 us
    all_gather x2, blocking collectives, prefix(): pieces = jax.tree.map(lambda part: lax.all_gather(part, axis), value)  21.4 us
    ppermute x4, starting transfers between devices, padded_2(): lax.ppermute(tail, axis, [(i, (i + 1) % count) for i in range(ends)])  16.6 us
    psum x1, blocking collectives, on_device(): lax.psum(lax.psum(content, named_axis), bus_axis)  15.4 us
    dot_general x18, matrix products, kernel_grad(): lax.dot_general(piece, flat_grad, (((0,), (0,)), ((), ())), preferred_ele...  11.7 us
  transfers between devices with their start and end apart: 9, of which 1 were waited for; matrix products, arithmetic and copies ran while one was open for 2% of the time, Pallas kernels for 0%

profile of v1, /device:TPU:8, one launch (start us, length us, event | category | flops | bytes accessed | tf_op | source)
XLA Modules:
  0.0 551.8 jit_solution(13605099137912416305)
XLA Ops:
  7.2 1.0 fusion.179
  8.2 3.8 collective-permute-start
  12.0 1.3 collective-permute-start.1
  13.3 0.7 reduce_window_sum.11
  14.7 8.7 %all-gather = f32[8,1,128]{2,1,0:T(1,128)S(1)} all-gather(f32[1,1,128]{2,1,0:T(1,128)S(1)} %get-tuple-element.381), channel_id=1, replica_groups=mesh['tm'=8,'rows'=8,'dp'=4] {'tm'}, dimensions={0}, use_global_device_ids=true | all-gather | bytes 4608 | tf_op jit(solution)/shard_map/all_gather | solution.py:27
  23.5 1.6 fusion.27
  29.0 4.5 copy.179
  33.5 8.3 %fusion.21 = f32[128,4,32,16]{2,3,1,0:T(8,128)} fusion(f32[16,4,32,128]{2,0,1,3:T(8,128)} %copy.179, f32[16,128]{0,1:T(8,128)S(1)} %copy.177, pred[16,16]{0,1:T(8,128)(4,1)S(1)} %iota_compare_fusion.2), kind=kOutput, calls=%fused_computation.80 | convolution fusion | flops 50429952 | bytes 2105600 | tf_op jit(solution)/shard_map/tkp,skrcp->strcp/dot_general | solution.py:126
  41.8 3.7 copy.181
  45.6 12.7 %all_gather.16 = f32[8,1,4,32,128]{4,3,2,1,0:T(8,128)S(1)} all-gather(f32[1,1,4,32,128]{4,3,2,1,0:T(8,128)S(1)} %slice.319), channel_id=1, replica_groups=mesh['tm'=8,'rows'=8,'dp'=4] {'tm'}, dimensions={0}, use_global_device_ids=true | all-gather | bytes 589824 | tf_op jit(solution)/shard_map/all_gather | solution.py:27
  58.7 2.4 fusion.171
  61.1 4.6 collective-permute-start.2
  65.7 1.3 collective-permute-start.3
  67.0 11.1 %all-gather.1 = bf16[8,1,128]{2,1,0:T(2,128)(2,1)S(1)} all-gather(bf16[1,1,128]{2,1,0:T(2,128)(2,1)S(1)} %get-tuple-element.380), channel_id=1, replica_groups=mesh['tm'=8,'rows'=8,'dp'=4] {'tm'}, dimensions={0}, use_global_device_ids=true | all-gather | bytes 2304 | tf_op jit(solution)/shard_map/all_gather | solution.py:42
  78.7 2.2 slice.346
  85.1 0.7 copy-done.12
  85.9 2.3 fusion.8
  88.2 1.0 convolution_bitcast_fusion.7
  89.2 1.0 convolution_bitcast_fusion.3
  90.2 1.0 convolution_bitcast_fusion.5
  91.2 1.0 convolution_bitcast_fusion.6
  92.1 1.0 convolution_bitcast_fusion.8
  93.1 1.0 convolution_bitcast_fusion.4
  94.0 1.0 convolution_bitcast_fusion.1
  95.0 1.0 convolution_bitcast_fusion
  96.0 1.0 convolution_bitcast_fusion.2
  97.0 4.5 collective-permute-start.4
  101.6 1.3 collective-permute-start.5
  102.9 80.3 %psum.37 = f32[128]{0:T(128)S(1)} all-reduce(f32[128]{0:T(128)S(1)} %copy-done.25), channel_id=1, replica_groups=mesh['tm'=8,'rows'=8,'dp'=4] {'tm','rows','dp'}, use_global_device_ids=true, to_apply=%region_8.9 | all-reduce | flops 128 | bytes 1024 | tf_op jit(solution)/shard_map/psum | solution.py:165
  183.7 0.9 maximum_bitcast_fusion.5
  184.7 0.9 pad_maximum_fusion.1
  189.8 4.5 copy.182
  194.3 8.2 %fusion.19 = f32[128,4,32,16]{2,3,1,0:T(8,128)} fusion(f32[16,4,32,128]{2,0,1,3:T(8,128)} %copy.182, f32[16,128]{0,1:T(8,128)S(1)} %copy.177, pred[16,16]{0,1:T(8,128)(4,1)S(1)} %copy-done.21), kind=kOutput, calls=%fused_computation.78 | convolution fusion | flops 50429952 | bytes 2105600 | tf_op jit(solution)/shard_map/tkp,strcp->skrcp/dot_general | solution.py:143
  202.5 3.7 copy.183
  206.2 13.1 %all_gather.18 = bf16[8,1,4,32,128]{4,3,2,1,0:T(8,128)(2,1)S(1)} all-gather(bf16[1,1,4,32,128]{4,3,2,1,0:T(8,128)(2,1)S(1)} %fusion.73), channel_id=1, replica_groups=mesh['tm'=8,'rows'=8,'dp'=4] {'tm'}, dimensions={0}, use_global_device_ids=true | all-gather | bytes 294912 | tf_op jit(solution)/shard_map/all_gather | solution.py:42
  219.3 5.9 %while.31 = (s32[]{:T(128)}, f32[1,4,32,128]{3,2,1,0:T(8,128)S(1)}, s32[]{:T(128)}, bf16[8,128]{1,0:T(8,128)(2,1)}, bf16[8,1,4,32,128]{4,3,2,1,0:T(8,128)(2,1)S(...) while((s32[]{:T(128)}, f32[1,4,32,128]{3,2,1,0:T(8,128)S(1)}, s32[]{:T(128)}, ...), condition=%wide.region_4.5_spmd.clone, body=%wide.region_3.4_spmd.clone.sunk | while | flops 82056 | bytes 165287 | solution.py:60
  220.1 0.7 bitcast_convert_fusion.2
  225.2 1.5 fusion.18
  230.3 3.6 collective-permute-start.6
  233.9 1.3 collective-permute-start.7
  235.3 31.2 %psum.38 = f32[16,128]{0,1:T(8,128)S(1)} all-reduce(f32[16,128]{0,1:T(8,128)S(1)} %copy.211), channel_id=1, replica_groups=mesh['tm'=8,'rows'=8,'dp'=4] {'rows'}, use_global_device_ids=true, to_apply=%region_10.11 | all-reduce | flops 2048 | bytes 16384 | tf_op jit(solution)/shard_map/psum | solution.py:158
  266.5 15.4 %psum.39 = f32[16,128]{0,1:T(8,128)S(1)} all-reduce(f32[16,128]{0,1:T(8,128)S(1)} %psum.38), channel_id=1, replica_groups=mesh['tm'=8,'rows'=8,'dp'=4] {'dp'}, use_global_device_ids=true, to_apply=%region_11.12 | all-reduce | flops 2048 | bytes 16384 | tf_op jit(solution)/shard_map/psum | solution.py:157
  282.6 0.9 pad_maximum_fusion
  287.8 0.9 copy-done.2
  288.7 1.0 add_convert_fusion
  289.8 251.1 %all-reduce.7.cloned.1.call-done = (f32[3,3,128,128]{3,2,1,0:T(8,128)}, f32[3,3,128,128]{3,2,1,0:T(8,128)}) async-done(((f32[3,3,128,128]{3,2,1,0:T(8,128)}, f32[3,3,128,128]{3,2,1,0:T(8,128)}), (f32[3,3,128,128]{3,2,1,0:T(8,128)}, f32[3,3,128,128]{3,2,1,0:T(8,128)})) %all-reduce.7.cloned.1.call-update) | async-done | bytes 1179664 | tf_op jit(solution)/shard_map/psum | solution.py:165
  540.9 1.9 broadcast_multiply_fusion
  542.8 1.9 broadcast_multiply_fusion.1
  (167 shorter events, 28.2 us)
Async XLA Ops:
  7.2 533.7 %all-reduce.7.cloned.1.call-start = ((), (), s32[]{:S(2)}) async-start(), calls=%async_computation | async-start | bytes 2359296 | tf_op jit(solution)/shard_map/psum | solution.py:165
  8.2 15.2 %collective-permute-start = (bf16[1,16,1,32,128]{4,3,2,1,0:T(8,128)(2,1)S(1)}, bf16[1,16,1,32,128]{4,3,2,1,0:T(8,128)(2,1)S(1)}, u32[]{:S(2)}, u32[]{:S(2)}) collective-permute-start(bf16[1,16,1,32,128]{4,3,2,1,0:T(8,128)(2,1)S(1)} %get-tuple-element.375), channel_id=1, source_target_pairs={{0,4},{4,8},{8,12},{12,16},{16,20},{20,24},{24,28},{1,5},{5,9},{9,... | collective-permute-start | bytes 393224 | tf_op jit(solution)/shard_map/ppermute | solution.py:16
  12.0 11.4 %collective-permute-start.1 = (bf16[1,16,1,32,128]{4,3,2,1,0:T(8,128)(2,1)S(1)}, bf16[1,16,1,32,128]{4,3,2,1,0:T(8,128)(2,1)S(1)}, u32[]{:S(2)}, u32[]{:S(2)}) collective-permute-start(bf16[1,16,1,32,128]{4,3,2,1,0:T(8,128)(2,1)S(1)} %get-tuple-element.376), channel_id=1, source_target_pairs={{4,0},{8,4},{12,8},{16,12},{20,16},{24,20},{28,24},{5,1},{9,5},{13... | collective-permute-start | bytes 393224 | tf_op jit(solution)/shard_map/ppermute | solution.py:18
  23.4 10.1 %copy-start.20 = (pred[16,16]{0,1:T(8,128)(4,1)}, pred[16,16]{0,1:T(8,128)(4,1)S(1)}, u32[]{:S(2)}) copy-start(pred[16,16]{0,1:T(8,128)(4,1)S(1)} %iota_compare_fusion.2) | copy-start | bytes 772
  25.1 1.0 copy-start.10
  25.7 1.1 copy-start
  26.8 0.8 copy-start.6
  26.8 1.9 copy-start.4
  45.6 13.1 %copy-start.3 = (f32[128,4,32,16]{0,2,1,3:T(8,128)}, f32[128,4,32,16]{0,2,1,3:T(8,128)S(1)}, u32[]{:S(2)}) copy-start(f32[128,4,32,16]{0,2,1,3:T(8,128)S(1)} %copy.181) | copy-start | bytes 3145732
  58.3 8.7 %copy-start.19 = (f32[16,128]{1,0:T(8,128)S(1)}, f32[16,128]{1,0:T(8,128)}, u32[]{:S(2)}) copy-start(f32[16,128]{1,0:T(8,128)} %param.15) | copy-start | bytes 24580
  61.1 19.9 %collective-permute-start.2 = (bf16[1,16,1,32,128]{4,3,2,1,0:T(8,128)(2,1)S(1)}, bf16[1,16,1,32,128]{4,3,2,1,0:T(8,128)(2,1)S(1)}, u32[]{:S(2)}, u32[]{:S(2)}) collective-permute-start(bf16[1,16,1,32,128]{4,3,2,1,0:T(8,128)(2,1)S(1)} %get-tuple-element.371), channel_id=1, source_target_pairs={{0,4},{4,8},{8,12},{12,16},{16,20},{20,24},{24,28},{1,5},{5,9},{9,... | collective-permute-start | bytes 393224 | tf_op jit(solution)/shard_map/ppermute | solution.py:16
  65.7 15.3 %collective-permute-start.3 = (bf16[1,16,1,32,128]{4,3,2,1,0:T(8,128)(2,1)S(1)}, bf16[1,16,1,32,128]{4,3,2,1,0:T(8,128)(2,1)S(1)}, u32[]{:S(2)}, u32[]{:S(2)}) collective-permute-start(bf16[1,16,1,32,128]{4,3,2,1,0:T(8,128)(2,1)S(1)} %get-tuple-element.372), channel_id=1, source_target_pairs={{4,0},{8,4},{12,8},{16,12},{20,16},{24,20},{28,24},{5,1},{9,5},{13... | collective-permute-start | bytes 393224 | tf_op jit(solution)/shard_map/ppermute | solution.py:18
  81.5 1.0 copy-start.8
  84.8 1.0 copy-start.12
  84.8 1.0 copy-start.23
  88.1 2.1 copy-start.1
  95.0 7.9 %copy-start.25 = (f32[128]{0:T(128)S(1)}, f32[128]{0:T(128)}, u32[]{:S(2)}) copy-start(f32[128]{0:T(128)} %get-tuple-element.330) | copy-start | bytes 1540
  95.0 88.7 %copy-start.13 = (f32[1,128,128]{2,1,0:T(8,128)S(1)}, f32[1,128,128]{2,1,0:T(8,128)}, u32[]{:S(2)}) copy-start(f32[1,128,128]{2,1,0:T(8,128)} %convolution_bitcast_fusion.7) | copy-start | bytes 196612
  95.0 88.7 %copy-start.14 = (f32[1,128,128]{2,1,0:T(8,128)S(1)}, f32[1,128,128]{2,1,0:T(8,128)}, u32[]{:S(2)}) copy-start(f32[1,128,128]{2,1,0:T(8,128)} %convolution_bitcast_fusion.3) | copy-start | bytes 196612
  95.0 88.7 %copy-start.15 = (f32[1,128,128]{2,1,0:T(8,128)S(1)}, f32[1,128,128]{2,1,0:T(8,128)}, u32[]{:S(2)}) copy-start(f32[1,128,128]{2,1,0:T(8,128)} %convolution_bitcast_fusion.5) | copy-start | bytes 196612
  95.0 88.7 %copy-start.16 = (f32[1,128,128]{2,1,0:T(8,128)S(1)}, f32[1,128,128]{2,1,0:T(8,128)}, u32[]{:S(2)}) copy-start(f32[1,128,128]{2,1,0:T(8,128)} %convolution_bitcast_fusion.6) | copy-start | bytes 196612
  95.0 88.7 %copy-start.17 = (f32[1,128,128]{2,1,0:T(8,128)S(1)}, f32[1,128,128]{2,1,0:T(8,128)}, u32[]{:S(2)}) copy-start(f32[1,128,128]{2,1,0:T(8,128)} %convolution_bitcast_fusion.8) | copy-start | bytes 196612
  95.0 88.7 %copy-start.18 = (f32[1,128,128]{2,1,0:T(8,128)S(1)}, f32[1,128,128]{2,1,0:T(8,128)}, u32[]{:S(2)}) copy-start(f32[1,128,128]{2,1,0:T(8,128)} %convolution_bitcast_fusion.4) | copy-start | bytes 196612
  97.0 88.5 %collective-permute-start.4 = (bf16[1,16,1,32,128]{4,3,2,1,0:T(8,128)(2,1)S(1)}, bf16[1,16,1,32,128]{4,3,2,1,0:T(8,128)(2,1)S(1)}, u32[]{:S(2)}, u32[]{:S(2)}) collective-permute-start(bf16[1,16,1,32,128]{4,3,2,1,0:T(8,128)(2,1)S(1)} %get-tuple-element.367), channel_id=1, source_target_pairs={{0,4},{4,8},{8,12},{12,16},{16,20},{20,24},{24,28},{1,5},{5,9},{9,... | collective-permute-start | bytes 393224 | tf_op jit(solution)/shard_map/ppermute | solution.py:16
  101.6 84.0 %collective-permute-start.5 = (bf16[1,16,1,32,128]{4,3,2,1,0:T(8,128)(2,1)S(1)}, bf16[1,16,1,32,128]{4,3,2,1,0:T(8,128)(2,1)S(1)}, u32[]{:S(2)}, u32[]{:S(2)}) collective-permute-start(bf16[1,16,1,32,128]{4,3,2,1,0:T(8,128)(2,1)S(1)} %get-tuple-element.368), channel_id=1, source_target_pairs={{4,0},{8,4},{12,8},{16,12},{20,16},{24,20},{28,24},{5,1},{9,5},{13... | collective-permute-start | bytes 393224 | tf_op jit(solution)/shard_map/ppermute | solution.py:18
  186.0 1.0 copy-start.9
  189.8 4.5 copy-start.21
  202.5 3.7 copy-start.22
  227.1 1.0 copy-start.5
  227.4 1.1 copy-start.7
  230.3 53.3 %collective-permute-start.6 = (bf16[1,16,1,32,128]{4,3,2,1,0:T(8,128)(2,1)S(1)}, bf16[1,16,1,32,128]{4,3,2,1,0:T(8,128)(2,1)S(1)}, u32[]{:S(2)}, u32[]{:S(2)}) collective-permute-start(bf16[1,16,1,32,128]{4,3,2,1,0:T(8,128)(2,1)S(1)} %get-tuple-element.363), channel_id=1, source_target_pairs={{0,4},{4,8},{8,12},{12,16},{16,20},{20,24},{24,28},{1,5},{5,9},{9,... | collective-permute-start | bytes 393224 | tf_op jit(solution)/shard_map/ppermute | solution.py:16
  233.9 49.6 %collective-permute-start.7 = (bf16[1,16,1,32,128]{4,3,2,1,0:T(8,128)(2,1)S(1)}, bf16[1,16,1,32,128]{4,3,2,1,0:T(8,128)(2,1)S(1)}, u32[]{:S(2)}, u32[]{:S(2)}) collective-permute-start(bf16[1,16,1,32,128]{4,3,2,1,0:T(8,128)(2,1)S(1)} %get-tuple-element.364), channel_id=1, source_target_pairs={{4,0},{8,4},{12,8},{16,12},{20,16},{24,20},{28,24},{5,1},{9,5},{13... | collective-permute-start | bytes 393224 | tf_op jit(solution)/shard_map/ppermute | solution.py:18
  284.1 1.0 copy-start.11
  287.5 1.2 copy-start.2
  287.5 1.2 copy-start.24
Sparse Core Ops, SparseCore 0:
  283.7 257.1 all-reduce.6
